TPU v7x, 32 devices: a whole 2x2x4 slice. The times are simulated.
32 devices in a mesh: head: 2 (over y), seq: 16 (over z, x, core).
Axes of the slice: x: 2, y: 2, z: 4, core: 2. Of those that a mesh axis runs over, the one named last changes fastest.
Arguments:
- queries: bfloat16 [2, 8192, 2, 256], P(None, 'seq', 'head'), may hold values from -5 to 5
- key_rows: bfloat16 [2, 8192, 2, 256], P(None, 'seq', 'head'), may hold values from -5 to 5
- values: bfloat16 [2, 8192, 2, 256], P(None, 'seq', 'head'), may hold values from -6 to 6
- learn_rates: float32 [2, 2, 8192], P('head', None, 'seq'), may hold values from 0.02 to 0.6, as said below
- fast_gate: float32 [2, 256, 512], P('head'), may hold values from -0.375 to 0.375
- fast_down: float32 [2, 512, 256], P('head'), may hold values from -0.25 to 0.25
- fast_up: float32 [2, 256, 512], P('head'), may hold values from -0.375 to 0.375
- output_weight: bfloat16 [512, 512], P(None, ('head', 'seq')), may hold values from -0.25 to 0.25
Outputs:
- output: bfloat16 [2, 8192, 512], P(None, 'seq', 'head')
Inputs may be any that keep to these rules, and one draw needn't show every extreme that they name: `learn_rates`: learning rates are positive.
All inputs are finite; a program needn't handle non-finite values.
Results may differ from a plain program's by a relative error of at most 0.0095.
Values may be sent and summed in bfloat16 or wider, within the bound.
A program may use at most 64 MiB of HBM per device.

v0:
```python
import functools
import math

import jax
import jax.numpy as jnp
from jax import lax
from jax.experimental import pallas as pl
from jax.experimental.pallas import tpu as pltpu
from jax.sharding import PartitionSpec as P

WINDOW = 256
MOMENTUM = 0.9
LANES = 128
MESH = pl.DeviceIdType.MESH
F32 = jnp.float32
BF16 = jnp.bfloat16


def radices_of(count):
    found = []
    while count > 1:
        if count % 2:
            found.append(count)
        elif len(found) < 2 or count % 4:
            found.append(2)
        else:
            found.append(4)
        count //= found[-1]
    return found


def dot(left, right):
    return jnp.dot(left, right, preferred_element_type=F32)


def dot_t(left, right):
    return lax.dot_general(left, right, (((1,), (1,)), ((), ())), preferred_element_type=F32)


def sigmoid(value):
    return 0.5 * jnp.tanh(0.5 * value) + 0.5


def kernel(
    n_seq, n_head, gather_weight,
    q_hbm, k_hbm, v_hbm, rate_hbm, gate_hbm, down_hbm, up_hbm, ow_hbm,
    out_ref,
    q_ref, k_ref, v_ref, rate_ref, gate_w, down_ref, up_w, ow_ref, down_w,
    mom, gate_b, up_b, down_tb, keys_t, target, target_t, hid_s, da_s, db_s,
    acc, send_b, recv_b, full_b, edge_k, edge_v, ow_all, ow_t, mix, win,
    load_sem, ar_send, ar_recv, ag_send, ag_recv, halo_send, halo_recv, ow_send, ow_recv, mix_send, mix_recv,
):
    spans, rows, dh = q_ref.shape
    hid = gate_w.shape[1]
    cols = hid // LANES
    part_rows = cols * dh
    wts = (gate_w, down_w, up_w)
    current = (gate_b, down_tb, up_b)
    radices = radices_of(n_seq)
    levels = len(radices)
    me = lax.axis_index("seq")
    head = lax.axis_index("head")

    loads = {}

    def load(name, source, dest):
        loads[name] = pltpu.make_async_copy(source, dest, load_sem.at[len(loads)])
        loads[name].start()

    load("gate", gate_hbm, gate_w)
    load(("k", 0), k_hbm.at[0], k_ref.at[0])
    load("up", up_hbm, up_w)
    load("rate", rate_hbm, rate_ref)
    load(("v", 0), v_hbm.at[0], v_ref.at[0])
    load("down", down_hbm, down_ref)
    load("ow", ow_hbm, ow_ref)
    for c in range(1, spans):
        load(("k", c), k_hbm.at[c], k_ref.at[c])
        load(("v", c), v_hbm.at[c], v_ref.at[c])
    load("q", q_hbm, q_ref)

    strides, digits = [], []
    stride = 1
    for radix in radices:
        strides.append(stride)
        digits.append(lax.rem(me // stride, radix))
        stride *= radix

    def peer(level, step):
        radix = radices[level]
        other = lax.rem(digits[level] + step, radix)
        return me + (other - digits[level]) * strides[level], other

    following = lax.rem(me + 1, n_seq)
    before = lax.rem(me + n_seq - 1, n_seq)

    barrier = pltpu.get_barrier_semaphore()
    greeted = 0
    for level in range(levels):
        for step in range(1, radices[level]):
            pl.semaphore_signal(barrier, inc=1, device_id={"seq": peer(level, step)[0]}, device_id_type=MESH)
            greeted += 1
    for other in (following, before):
        pl.semaphore_signal(barrier, inc=1, device_id={"seq": other}, device_id_type=MESH)
        greeted += 1
    for step in range(1, n_head):
        pl.semaphore_signal(
            barrier, inc=1, device_id={"head": lax.rem(head + step, n_head)}, device_id_type=MESH
        )
        greeted += 1

    def prepare(c):
        rate_row = jnp.broadcast_to(rate_ref[c : c + 1, :], (LANES, rows))
        rate = rate_row.T
        rate = jnp.concatenate([rate] * (dh // LANES), axis=1)
        aim = (-(rate * v_ref[c].astype(F32))).astype(BF16)
        target[...] = aim
        target_t[...] = aim.T
        keys_t[...] = k_ref[c].T

    def gradient(c):
        piece = min(256, rows)
        for start in range(0, rows, piece):
            part = slice(start, start + piece)
            k_part = k_ref[c, part]
            pre_gate = dot(k_part, gate_b[...])
            pre_up = dot(k_part, up_b[...])
            back = dot(target[part, :], down_tb[...])
            sig = sigmoid(pre_gate)
            silu = pre_gate * sig
            hid_s[part, :] = (silu * pre_up).astype(BF16)
            da_s[part, :] = (back * pre_up * (sig * (1.0 + pre_gate * (1.0 - sig)))).astype(BF16)
            db_s[part, :] = (back * silu).astype(BF16)
        for p, (left, right) in enumerate(((target_t, hid_s), (keys_t, da_s), (keys_t, db_s))):
            grad = dot(left[...], right[...])
            for cb in range(cols):
                base = p * part_rows + cb * dh
                block = grad[:, cb * LANES : (cb + 1) * LANES]
                acc[base : base + dh, :] = block
                send_b[c, base : base + dh, :] = block.astype(BF16)
            start_stage(c, p, 0)

    def span_of(start, size):
        return pl.ds(pl.multiple_of(start, 16), size)

    def fill(work):
        if work:
            work.pop(0)()

    def owned(unit, level):
        start = 0
        for l in range(level + 1):
            start = start + digits[l] * (unit * math.prod(radices[l + 1 :]))
        return start

    def gather_copies(buf, offset, unit, level, sends, recvs):
        size = unit * math.prod(radices[level + 1 :])
        made = []
        for step in range(1, radices[level]):
            slot = sum(radices[:level]) + step
            block = buf.at[span_of(offset + owned(unit, level), size)]
            made.append(
                pltpu.make_async_remote_copy(
                    src_ref=block, dst_ref=block, send_sem=sends.at[slot], recv_sem=recvs.at[slot],
                    device_id={"seq": peer(level, step)[0]}, device_id_type=MESH,
                )
            )
        return made

    unit = part_rows // n_seq

    def scatter_copies(c, p, level):
        size = unit * math.prod(radices[level + 1 :])
        base = p * part_rows + (owned(unit, level - 1) if level else 0)
        made = []
        for step in range(1, radices[level]):
            target_dev, other = peer(level, step)
            slot = sum(radices[:level]) + step
            made.append(
                pltpu.make_async_remote_copy(
                    src_ref=send_b.at[c, span_of(base + other * size, size)],
                    dst_ref=recv_b.at[c, pl.ds(landing_at(p, level) + (step - 1) * size, size)],
                    send_sem=ar_send.at[c, p, slot], recv_sem=ar_recv.at[c, p, slot],
                    device_id={"seq": target_dev}, device_id_type=MESH,
                )
            )
        return made

    def landing_at(p, level):
        sizes = [unit * math.prod(radices[l + 1 :]) * (radices[l] - 1) for l in range(levels)]
        return p * sum(sizes) + sum(sizes[:level])

    stages = 2 * levels

    def stage_copies(c, p, stage):
        if stage < levels:
            return scatter_copies(c, p, stage)
        return gather_copies(
            full_b.at[c], p * part_rows, unit, stages - 1 - stage, ag_send.at[c, p], ag_recv.at[c, p]
        )

    def start_stage(c, p, stage):
        for copy in stage_copies(c, p, stage):
            copy.start()

    def finish_stage(c, p, stage):
        for copy in stage_copies(c, p, stage):
            copy.wait_recv()
        if stage < levels:
            size = unit * math.prod(radices[stage + 1 :])
            place = span_of(p * part_rows + owned(unit, stage), size)
            mine = acc[place, :]
            landed = landing_at(p, stage)
            for step in range(radices[stage] - 1):
                mine += recv_b[c, landed + step * size : landed + (step + 1) * size, :].astype(F32)
            if stage < levels - 1:
                acc[place, :] = mine
                send_b[c, place, :] = mine.astype(BF16)
            else:
                full_b[c, place, :] = mine.astype(BF16)
        if stage + 1 < stages:
            start_stage(c, p, stage + 1)

    def all_reduce(c, work):
        squares = jnp.zeros((8, LANES), F32)
        for p in range(3):
            finish_stage(c, p, 0)
        for key in range(1, stages + 2):
            fill(work)
            for p in reversed(range(3)):
                stage = key - p
                if 1 <= stage < stages:
                    finish_stage(c, p, stage)
                    if stage == stages - 1:
                        for cb in range(cols):
                            base = p * part_rows + cb * dh
                            block = full_b[c, base : base + dh, :].astype(F32)
                            squares += jnp.sum((block * block).reshape(dh // 8, 8, LANES), axis=0)
        while work:
            fill(work)
        for p in range(3):
            for stage in range(stages):
                for copy in stage_copies(c, p, stage):
                    copy.wait_send()
        return squares

    def update(c, squares):
        whole = jnp.sum(jnp.sum(squares, axis=1, keepdims=True), axis=0, keepdims=True)
        factor = jnp.minimum(1.0, 0.6 * math.sqrt(hid) / jnp.sqrt(whole + 1e-6))
        for p, m in ((1, 0), (2, 2), (0, 1)):
            for cb in range(cols):
                base = p * part_rows + cb * dh
                lanes = slice(cb * LANES, (cb + 1) * LANES)
                change = factor * full_b[c, base : base + dh, :].astype(F32)
                if c > 0:
                    change = MOMENTUM * mom[m, :, lanes] + change
                fresh = wts[m][:, lanes] - change
                if c < spans - 1:
                    mom[m, :, lanes] = change
                    wts[m][:, lanes] = fresh
                current[m][:, lanes] = fresh.astype(BF16)

    row_ids = lax.broadcasted_iota(jnp.int32, (WINDOW, WINDOW), 0)
    col_ids = lax.broadcasted_iota(jnp.int32, (WINDOW, WINDOW), 1)
    scale = 1.0 / math.sqrt(dh)

    def attend(c, j):
        start = j * WINDOW
        here = slice(start, start + WINDOW)
        left_ok = col_ids > row_ids
        if j == 0:
            first = me == 0
            span = jnp.where(first, (c + spans - 1) % spans, c)
            left_k, left_v = edge_k[span], edge_v[span]
            if c == 0:
                left_ok = left_ok & jnp.logical_not(first)
        else:
            earlier = slice(start - WINDOW, start)
            left_k, left_v = k_ref[c, earlier], v_ref[c, earlier]
        query = q_ref[c, here]
        left = jnp.where(left_ok, dot_t(query, left_k) * scale, -1e30)
        right = jnp.where(col_ids <= row_ids, dot_t(query, k_ref[c, here]) * scale, -1e30)
        top = jnp.maximum(jnp.max(left, axis=1, keepdims=True), jnp.max(right, axis=1, keepdims=True))
        left = jnp.exp(left - top)
        right = jnp.exp(right - top)
        share = 1.0 / (jnp.sum(left, axis=1, keepdims=True) + jnp.sum(right, axis=1, keepdims=True))
        win[c, here] = dot((left * share).astype(BF16), left_v) + dot(
            (right * share).astype(BF16), v_ref[c, here]
        )

    half = WINDOW

    def mix_copies(c, j):
        made = []
        for step in range(1, n_head):
            block = mix.at[head, c, pl.ds(j * half, half)]
            made.append(
                pltpu.make_async_remote_copy(
                    src_ref=block, dst_ref=block,
                    send_sem=mix_send.at[c, j, step], recv_sem=mix_recv.at[c, j, step],
                    device_id={"head": lax.rem(head + step, n_head)}, device_id_type=MESH,
                )
            )
        return made

    def apply(c, j):
        part = slice(j * half, (j + 1) * half)
        query = q_ref[c, part]
        pre_gate = dot(query, gate_b[...])
        hidden = (pre_gate * sigmoid(pre_gate) * dot(query, up_b[...])).astype(BF16)
        fast = dot_t(hidden, down_tb[...])
        norm = fast * lax.rsqrt(jnp.mean(fast * fast, axis=-1, keepdims=True) + 1e-5)
        mix[head, c, part] = (norm + win[c, part]).astype(BF16)
        for copy in mix_copies(c, j):
            copy.start()

    def project(c, j):
        part = slice(j * half, (j + 1) * half)
        for copy in mix_copies(c, j):
            copy.wait()
        result = None
        for h in range(n_head):
            term = dot_t(mix[h, c, part], ow_t[:, h * dh : (h + 1) * dh])
            result = term if result is None else result + term
        out_ref[c, part] = result.astype(BF16)

    halo = []
    for index, (source, dest) in enumerate(((k_hbm, edge_k), (v_hbm, edge_v))):
        for c in range(spans):
            halo.append(
                pltpu.make_async_remote_copy(
                    src_ref=source.at[c, pl.ds(rows - WINDOW, WINDOW)], dst_ref=dest.at[c],
                    send_sem=halo_send.at[index, c], recv_sem=halo_recv.at[index, c],
                    device_id={"seq": following}, device_id_type=MESH,
                )
            )

    shard = ow_ref.shape[0]

    def weight_copies(level):
        return gather_copies(ow_all, 0, shard, level, ow_send, ow_recv)

    def weight_next(level):
        if level < levels - 1:
            for copy in weight_copies(level + 1):
                copy.wait()
        for copy in weight_copies(level):
            copy.start()

    def weight_end():
        for copy in weight_copies(0):
            copy.wait()
        for s in range(n_seq):
            place, rest = 0, s
            for radix in radices:
                place = place * radix + rest % radix
                rest //= radix
            ow_t[s * shard : (s + 1) * shard, :] = ow_all[place * shard : (place + 1) * shard, :]

    tiles = rows // WINDOW
    pl.semaphore_wait(barrier, greeted)
    for copy in halo:
        copy.start()
    loads["gate"].wait()
    gate_b[...] = gate_w[...].astype(BF16)
    loads["up"].wait()
    up_b[...] = up_w[...].astype(BF16)
    loads["down"].wait()
    down_w[...] = down_ref[...].T
    down_tb[...] = down_w[...].astype(BF16)
    loads["rate"].wait()
    loads[("k", 0)].wait()
    loads[("v", 0)].wait()
    prepare(0)
    loads["ow"].wait()
    if gather_weight:
        ow_all[span_of(owned(shard, levels - 1), shard), :] = ow_ref[...]
        weight_next(levels - 1)
    else:
        ow_t[...] = ow_ref[...]
    gradient(0)
    loads["q"].wait()
    for c in range(1, spans):
        loads[("k", c)].wait()
        loads[("v", c)].wait()
    for c in range(spans):
        work = []
        if c + 1 < spans:
            work.append(functools.partial(prepare, c + 1))
        if c == 0:
            work += [functools.partial(attend, s, j) for s in range(spans) for j in range(1, tiles)]

            def edges():
                for copy in halo:
                    copy.wait()
                attend(0, 0)

            work.append(edges)
            work += [functools.partial(attend, s, 0) for s in range(1, spans)]
        if c > 0:
            work += [functools.partial(apply, c - 1, j) for j in range(tiles)]
        if c == spans - 1:
            if gather_weight:
                first = levels - 2 if c > 0 else levels - 1
                work += [functools.partial(weight_next, level) for level in reversed(range(first))]
                work.append(weight_end)
            work += [functools.partial(project, s, j) for s in range(c) for j in range(tiles)]
        update(c, all_reduce(c, work))
        if c + 1 < spans:
            if c + 1 == spans - 1 and gather_weight and levels > 1:
                weight_next(levels - 2)
            gradient(c + 1)
    for j in range(tiles):
        apply(spans - 1, j)
    for j in range(tiles):
        project(spans - 1, j)


def body(n_seq, n_head, queries, key_rows, values, learn_rates, fast_gate, fast_down, fast_up, output_weight):
    spans, rows, _, dh = queries.shape
    hid = fast_gate.shape[2]
    features, shard = output_weight.shape
    gather_weight = shard % 16 == 0
    if gather_weight:
        weight = output_weight.T
    else:
        weight = lax.all_gather(output_weight, "seq", axis=1, tiled=True).T
    out_cols = shard * n_seq
    cols = hid // LANES
    total = 3 * cols * dh
    radices = radices_of(n_seq)
    landing, size = 0, total
    for radix in radices:
        size //= radix
        landing += (radix - 1) * size
    slots = sum(radices) + 1
    tiles = rows // WINDOW
    dma = pltpu.SemaphoreType.DMA
    vmem = pltpu.VMEM
    return pl.pallas_call(
        functools.partial(kernel, n_seq, n_head, gather_weight),
        out_shape=jax.ShapeDtypeStruct((spans, rows, out_cols), BF16),
        in_specs=[pl.BlockSpec(memory_space=pltpu.HBM)] * 8,
        out_specs=pl.BlockSpec(memory_space=pltpu.VMEM),
        scratch_shapes=[
            vmem((spans, rows, dh), BF16),
            vmem((spans, rows, dh), BF16),
            vmem((spans, rows, dh), BF16),
            vmem((spans, rows), F32),
            vmem((dh, hid), F32),
            vmem((hid, dh), F32),
            vmem((dh, hid), F32),
            vmem(weight.shape, BF16),
            vmem((dh, hid), F32),
            vmem((3, dh, hid), F32),
            vmem((dh, hid), BF16),
            vmem((dh, hid), BF16),
            vmem((dh, hid), BF16),
            vmem((dh, rows), BF16),
            vmem((rows, dh), BF16),
            vmem((dh, rows), BF16),
            vmem((rows, hid), BF16),
            vmem((rows, hid), BF16),
            vmem((rows, hid), BF16),
            vmem((total, LANES), F32),
            vmem((spans, total, LANES), BF16),
            vmem((spans, landing, LANES), BF16),
            vmem((spans, total, LANES), BF16),
            vmem((spans, WINDOW, dh), BF16),
            vmem((spans, WINDOW, dh), BF16),
            vmem((out_cols, features), BF16),
            vmem((out_cols, features), BF16),
            vmem((n_head, spans, rows, dh), BF16),
            vmem((spans, rows, dh), F32),
            dma((6 + 2 * spans,)),
            dma((spans, 3, slots)),
            dma((spans, 3, slots)),
            dma((spans, 3, slots)),
            dma((spans, 3, slots)),
            dma((2, spans)),
            dma((2, spans)),
            dma((slots,)),
            dma((slots,)),
            dma((spans, tiles, n_head)),
            dma((spans, tiles, n_head)),
        ],
        compiler_params=pltpu.CompilerParams(
            collective_id=0, has_side_effects=True, vmem_limit_bytes=60 * 1024 * 1024
        ),
    )(
        queries[:, :, 0, :], key_rows[:, :, 0, :], values[:, :, 0, :], learn_rates[0],
        fast_gate[0], fast_down[0], fast_up[0], weight,
    )


def solution(mesh):
    placed = (
        P(None, "seq", "head", None),
        P(None, "seq", "head", None),
        P(None, "seq", "head", None),
        P("head", None, "seq"),
        P("head", None, None),
        P("head", None, None),
        P("head", None, None),
        P(None, ("head", "seq")),
    )
    return jax.shard_map(
        functools.partial(body, mesh.shape["seq"], mesh.shape["head"]),
        mesh=mesh, in_specs=placed, out_specs=P(None, "seq", "head"), check_vma=False,
    )
```

profile of v0, /device:TPU:0, one launch (start us, length us, event | category | flops | bytes accessed | tf_op | source)
XLA Modules:
  0.0 69.6 jit_solution(12440627669296566048)
XLA Ops:
  0.0 67.8 %shard_map.82 = bf16[2,512,256]{2,1,0:T(8,128)(2,1)} custom-call(bf16[2,512,256]{2,1,0:T(8,128)(2,1)} %bitcast.8, bf16[2,512,256]{2,1,0:T(8,128)(2,1)} %bitcast.9, bf16[2,512,256]{2,1,0:T(8,128)(2,1)} %bitcast.10, f32[2,512]{1,0:T(2,128)} %bitcast.15, f32[256,512]{1,0:T(8,128)} %bitcast.11, f32[512,256]{1,0:T(8,128)} %bitcast.12, f32[256,512]{1,0:T(8,128)} %bitcast.13, ...), custom_call_target="tpu_custom_call" | custom-call | tf_op jit(solution)/shard_map/pallas_call | solution.py:440
  67.8 1.9 %copy.10 = bf16[2,512,256]{2,1,0:T(8,128)(2,1)} copy(bf16[2,512,256]{2,1,0:T(8,128)(2,1)} %shard_map.82) | data formatting | bytes 1048576
where the time goes:
time: 69.8 us; the launch traced here: 69.6 us
  Pallas kernels  67.8 us (97%)
  local copies, waits for them, and re-layouts  1.87 us (3%)
    pallas_call x1, Pallas kernels, body(): pl.pallas_call(functools.partial(kernel, n_seq, n_head, gather_weight), o...  67.8 us
    unnamed x1, local copies, waits for them, and re-layouts  1.87 us

commit v1 on v0

--- a/solution.py
+++ b/solution.py
@@ -46,20 +46,22 @@
     q_hbm, k_hbm, v_hbm, rate_hbm, gate_hbm, down_hbm, up_hbm, ow_hbm,
     out_ref,
     q_ref, k_ref, v_ref, rate_ref, gate_w, down_ref, up_w, ow_ref, down_w,
-    mom, gate_b, up_b, down_tb, keys_t, target, target_t, hid_s, da_s, db_s,
-    acc, send_b, recv_b, full_b, edge_k, edge_v, ow_all, ow_t, mix, win,
-    load_sem, ar_send, ar_recv, ag_send, ag_recv, halo_send, halo_recv, ow_send, ow_recv, mix_send, mix_recv,
+    mom, start_b, cur, keys_t, target, target_t, k_far, target_far, hid_s, da_s, db_s,
+    acc, send_b, recv_b, full_b, sq_out, sq_in, edge_k, edge_v, ow_all, ow_t, mix, win, near,
+    load_sem, pair_send, pair_recv, cur_send, cur_recv, sq_send, sq_recv, ar_send, ar_recv, ag_send, ag_recv, halo_send, halo_recv, ow_send, ow_recv, mix_send, mix_recv,
 ):
     spans, rows, dh = q_ref.shape
-    hid = gate_w.shape[1]
-    cols = hid // LANES
+    hid = gate_hbm.shape[1]
+    ways = radices_of(n_seq)[0]
+    hid_part = hid // ways
+    cols = hid_part // LANES
     part_rows = cols * dh
     wts = (gate_w, down_w, up_w)
-    current = (gate_b, down_tb, up_b)
     radices = radices_of(n_seq)
     levels = len(radices)
     me = lax.axis_index("seq")
     head = lax.axis_index("head")
+    share = pl.ds(pl.multiple_of(lax.rem(me, ways) * hid_part, hid_part), hid_part)
 
     loads = {}
 
@@ -67,12 +69,12 @@
         loads[name] = pltpu.make_async_copy(source, dest, load_sem.at[len(loads)])
         loads[name].start()
 
-    load("gate", gate_hbm, gate_w)
+    load("gate", gate_hbm.at[:, share], gate_w)
     load(("k", 0), k_hbm.at[0], k_ref.at[0])
-    load("up", up_hbm, up_w)
+    load("up", up_hbm.at[:, share], up_w)
     load("rate", rate_hbm, rate_ref)
     load(("v", 0), v_hbm.at[0], v_ref.at[0])
-    load("down", down_hbm, down_ref)
+    load("down", down_hbm.at[share], down_ref)
     load("ow", ow_hbm, ow_ref)
     for c in range(1, spans):
         load(("k", c), k_hbm.at[c], k_ref.at[c])
@@ -91,6 +93,13 @@
         other = lax.rem(digits[level] + step, radix)
         return me + (other - digits[level]) * strides[level], other
 
+    def near_peer(step):
+        width = ways * radices[1] if levels > 1 else ways
+        spot = lax.rem(me, width)
+        return me + lax.rem(spot + step, width) - spot
+
+    near_steps = range(1, ways * (radices[1] if levels > 1 else 1))
+
     following = lax.rem(me + 1, n_seq)
     before = lax.rem(me + n_seq - 1, n_seq)
 
@@ -100,6 +109,9 @@
         for step in range(1, radices[level]):
             pl.semaphore_signal(barrier, inc=1, device_id={"seq": peer(level, step)[0]}, device_id_type=MESH)
             greeted += 1
+    for step in near_steps:
+        pl.semaphore_signal(barrier, inc=1, device_id={"seq": near_peer(step)}, device_id_type=MESH)
+        greeted += 1
     for other in (following, before):
         pl.semaphore_signal(barrier, inc=1, device_id={"seq": other}, device_id_type=MESH)
         greeted += 1
@@ -114,25 +126,55 @@
         rate = rate_row.T
         rate = jnp.concatenate([rate] * (dh // LANES), axis=1)
         aim = (-(rate * v_ref[c].astype(F32))).astype(BF16)
-        target[...] = aim
-        target_t[...] = aim.T
-        keys_t[...] = k_ref[c].T
+        target[c] = aim
+        for copy in pair_copies(c, 1):
+            copy.start()
+        target_t[c, :, :rows] = aim.T
+        keys_t[c, :, :rows] = k_ref[c].T
+
+    def pair_copies(c, kind):
+        made = []
+        for step in range(1, ways):
+            source, dest = ((k_hbm, k_far), (target, target_far))[kind]
+            made.append(
+                pltpu.make_async_remote_copy(
+                    src_ref=source.at[c], dst_ref=dest.at[c, step - 1],
+                    send_sem=pair_send.at[c, kind, step], recv_sem=pair_recv.at[c, kind, step],
+                    device_id={"seq": peer(0, step)[0]}, device_id_type=MESH,
+                )
+            )
+        return made
+
+    def prepare_far(c):
+        for kind in range(2):
+            for copy in pair_copies(c, kind):
+                copy.wait()
+        for step in range(1, ways):
+            place = slice(step * rows, (step + 1) * rows)
+            target_t[c, :, place] = target_far[c, step - 1].T
+            keys_t[c, :, place] = k_far[c, step - 1].T
 
     def gradient(c):
+        weights = start_b if c == 0 else cur.at[c - 1, 0]
         piece = min(256, rows)
-        for start in range(0, rows, piece):
-            part = slice(start, start + piece)
-            k_part = k_ref[c, part]
-            pre_gate = dot(k_part, gate_b[...])
-            pre_up = dot(k_part, up_b[...])
-            back = dot(target[part, :], down_tb[...])
-            sig = sigmoid(pre_gate)
-            silu = pre_gate * sig
-            hid_s[part, :] = (silu * pre_up).astype(BF16)
-            da_s[part, :] = (back * pre_up * (sig * (1.0 + pre_gate * (1.0 - sig)))).astype(BF16)
-            db_s[part, :] = (back * silu).astype(BF16)
+        for slot in range(ways):
+            if c == 0 and slot == 1:
+                prepare_far(c)
+            for start in range(0, rows, piece):
+                part = slice(start, start + piece)
+                place = slice(slot * rows + start, slot * rows + start + piece)
+                k_part = k_ref[c, part] if slot == 0 else k_far[c, slot - 1, part]
+                aim = target[c, part] if slot == 0 else target_far[c, slot - 1, part]
+                pre_gate = dot(k_part, weights[0])
+                pre_up = dot(k_part, weights[2])
+                back = dot(aim, weights[1])
+                sig = sigmoid(pre_gate)
+                silu = pre_gate * sig
+                hid_s[place, :] = (silu * pre_up).astype(BF16)
+                da_s[place, :] = (back * pre_up * (sig * (1.0 + pre_gate * (1.0 - sig)))).astype(BF16)
+                db_s[place, :] = (back * silu).astype(BF16)
         for p, (left, right) in enumerate(((target_t, hid_s), (keys_t, da_s), (keys_t, db_s))):
-            grad = dot(left[...], right[...])
+            grad = dot(left[c], right[...])
             for cb in range(cols):
                 base = p * part_rows + cb * dh
                 block = grad[:, cb * LANES : (cb + 1) * LANES]
@@ -147,18 +189,18 @@
         if work:
             work.pop(0)()
 
-    def owned(unit, level):
+    def owned(unit, level, first):
         start = 0
-        for l in range(level + 1):
+        for l in range(first, level + 1):
             start = start + digits[l] * (unit * math.prod(radices[l + 1 :]))
         return start
 
-    def gather_copies(buf, offset, unit, level, sends, recvs):
+    def gather_copies(buf, offset, unit, level, first, sends, recvs):
         size = unit * math.prod(radices[level + 1 :])
         made = []
         for step in range(1, radices[level]):
             slot = sum(radices[:level]) + step
-            block = buf.at[span_of(offset + owned(unit, level), size)]
+            block = buf.at[span_of(offset + owned(unit, level, first), size)]
             made.append(
                 pltpu.make_async_remote_copy(
                     src_ref=block, dst_ref=block, send_sem=sends.at[slot], recv_sem=recvs.at[slot],
@@ -167,11 +209,15 @@
             )
         return made
 
-    unit = part_rows // n_seq
+    unit = part_rows // (n_seq // ways)
+
+    def landing_at(p, level):
+        sizes = [unit * math.prod(radices[l + 1 :]) * (radices[l] - 1) for l in range(1, levels)]
+        return p * sum(sizes) + sum(sizes[: level - 1])
 
     def scatter_copies(c, p, level):
         size = unit * math.prod(radices[level + 1 :])
-        base = p * part_rows + (owned(unit, level - 1) if level else 0)
+        base = p * part_rows + owned(unit, level - 1, 1)
         made = []
         for step in range(1, radices[level]):
             target_dev, other = peer(level, step)
@@ -186,63 +232,111 @@
             )
         return made
 
-    def landing_at(p, level):
-        sizes = [unit * math.prod(radices[l + 1 :]) * (radices[l] - 1) for l in range(levels)]
-        return p * sum(sizes) + sum(sizes[:level])
-
-    stages = 2 * levels
+    halfway = levels - 1
+    stages = 2 * halfway
 
     def stage_copies(c, p, stage):
-        if stage < levels:
-            return scatter_copies(c, p, stage)
+        if stage < halfway:
+            return scatter_copies(c, p, stage + 1)
         return gather_copies(
-            full_b.at[c], p * part_rows, unit, stages - 1 - stage, ag_send.at[c, p], ag_recv.at[c, p]
+            full_b.at[c], p * part_rows, unit, stages - stage, 1, ag_send.at[c, p], ag_recv.at[c, p]
         )
 
     def start_stage(c, p, stage):
         for copy in stage_copies(c, p, stage):
             copy.start()
 
+    def squares_of(value):
+        return jnp.sum((value * value).reshape(value.shape[0] // 8, 8, LANES), axis=0)
+
     def finish_stage(c, p, stage):
         for copy in stage_copies(c, p, stage):
             copy.wait_recv()
-        if stage < levels:
-            size = unit * math.prod(radices[stage + 1 :])
-            place = span_of(p * part_rows + owned(unit, stage), size)
+        squares = None
+        if stage < halfway:
+            level = stage + 1
+            size = unit * math.prod(radices[level + 1 :])
+            place = span_of(p * part_rows + owned(unit, level, 1), size)
             mine = acc[place, :]
-            landed = landing_at(p, stage)
-            for step in range(radices[stage] - 1):
+            landed = landing_at(p, level)
+            for step in range(radices[level] - 1):
                 mine += recv_b[c, landed + step * size : landed + (step + 1) * size, :].astype(F32)
-            if stage < levels - 1:
+            if level < levels - 1:
                 acc[place, :] = mine
                 send_b[c, place, :] = mine.astype(BF16)
             else:
                 full_b[c, place, :] = mine.astype(BF16)
         if stage + 1 < stages:
             start_stage(c, p, stage + 1)
+        if stage == halfway - 1:
+            squares = squares_of(mine)
+        return squares
+
+    def norm_copies(c, index):
+        level = levels - 1 - index
+        made = []
+        for step in range(1, radices[level]) if level > 1 else near_steps:
+            other = peer(level, step)[0] if level > 1 else near_peer(step)
+            made.append(
+                pltpu.make_async_remote_copy(
+                    src_ref=sq_out.at[c, index], dst_ref=sq_in.at[c, index, step],
+                    send_sem=sq_send.at[c, index, step], recv_sem=sq_recv.at[c, index, step],
+                    device_id={"seq": other}, device_id_type=MESH,
+                )
+            )
+        return made
+
+    def norm_start(c, index, squares):
+        sq_out[c, index] = squares
+        for copy in norm_copies(c, index):
+            copy.start()
+
+    def norm_finish(c, index):
+        squares = sq_out[c, index]
+        count = 1
+        for copy in norm_copies(c, index):
+            copy.wait()
+            squares = squares + sq_in[c, index, count]
+            count += 1
+        return squares
 
     def all_reduce(c, work):
-        squares = jnp.zeros((8, LANES), F32)
-        for p in range(3):
-            finish_stage(c, p, 0)
-        for key in range(1, stages + 2):
+        squares = None
+        for key in range(stages + 2):
             fill(work)
             for p in reversed(range(3)):
                 stage = key - p
-                if 1 <= stage < stages:
-                    finish_stage(c, p, stage)
-                    if stage == stages - 1:
-                        for cb in range(cols):
-                            base = p * part_rows + cb * dh
-                            block = full_b[c, base : base + dh, :].astype(F32)
-                            squares += jnp.sum((block * block).reshape(dh // 8, 8, LANES), axis=0)
+                if 0 <= stage < stages:
+                    term = finish_stage(c, p, stage)
+                    if term is not None:
+                        squares = term if squares is None else squares + term
+            if key >= halfway + 1:
+                index = key - halfway - 1
+                if index > 0:
+                    squares = norm_finish(c, index - 1)
+                if index < halfway:
+                    norm_start(c, index, squares)
         while work:
             fill(work)
+        return squares
+
+    def settle(c):
         for p in range(3):
             for stage in range(stages):
                 for copy in stage_copies(c, p, stage):
                     copy.wait_send()
-        return squares
+
+    def cur_copies(c):
+        made = []
+        for step in range(1, ways):
+            made.append(
+                pltpu.make_async_remote_copy(
+                    src_ref=cur.at[c, 0], dst_ref=cur.at[c, step],
+                    send_sem=cur_send.at[c, step], recv_sem=cur_recv.at[c, step],
+                    device_id={"seq": peer(0, step)[0]}, device_id_type=MESH,
+                )
+            )
+        return made
 
     def update(c, squares):
         whole = jnp.sum(jnp.sum(squares, axis=1, keepdims=True), axis=0, keepdims=True)
@@ -258,7 +352,9 @@
                 if c < spans - 1:
                     mom[m, :, lanes] = change
                     wts[m][:, lanes] = fresh
-                current[m][:, lanes] = fresh.astype(BF16)
+                cur[c, 0, m, :, lanes] = fresh.astype(BF16)
+        for copy in cur_copies(c):
+            copy.start()
 
     row_ids = lax.broadcasted_iota(jnp.int32, (WINDOW, WINDOW), 0)
     col_ids = lax.broadcasted_iota(jnp.int32, (WINDOW, WINDOW), 1)
@@ -303,16 +399,31 @@
             )
         return made
 
-    def apply(c, j):
+    def fast_part(c, j, slot):
+        query = q_ref[c, j * half : (j + 1) * half]
+        pre_gate = dot(query, cur[c, slot, 0])
+        hidden = (pre_gate * sigmoid(pre_gate) * dot(query, cur[c, slot, 2])).astype(BF16)
+        return dot_t(hidden, cur[c, slot, 1])
+
+    def apply_near(c, j):
+        near[c, j * half : (j + 1) * half] = fast_part(c, j, 0)
+
+    def apply_far(c, j):
         part = slice(j * half, (j + 1) * half)
-        query = q_ref[c, part]
-        pre_gate = dot(query, gate_b[...])
-        hidden = (pre_gate * sigmoid(pre_gate) * dot(query, up_b[...])).astype(BF16)
-        fast = dot_t(hidden, down_tb[...])
+        if j == 0:
+            for copy in cur_copies(c):
+                copy.wait()
+        fast = near[c, part]
+        for slot in range(1, ways):
+            fast = fast + fast_part(c, j, slot)
         norm = fast * lax.rsqrt(jnp.mean(fast * fast, axis=-1, keepdims=True) + 1e-5)
         mix[head, c, part] = (norm + win[c, part]).astype(BF16)
         for copy in mix_copies(c, j):
             copy.start()
+
+    def apply(c, j):
+        apply_near(c, j)
+        apply_far(c, j)
 
     def project(c, j):
         part = slice(j * half, (j + 1) * half)
@@ -338,7 +449,7 @@
     shard = ow_ref.shape[0]
 
     def weight_copies(level):
-        return gather_copies(ow_all, 0, shard, level, ow_send, ow_recv)
+        return gather_copies(ow_all, 0, shard, level, 0, ow_send, ow_recv)
 
     def weight_next(level):
         if level < levels - 1:
@@ -359,22 +470,26 @@
 
     tiles = rows // WINDOW
     pl.semaphore_wait(barrier, greeted)
-    for copy in halo:
-        copy.start()
-    loads["gate"].wait()
-    gate_b[...] = gate_w[...].astype(BF16)
-    loads["up"].wait()
-    up_b[...] = up_w[...].astype(BF16)
-    loads["down"].wait()
-    down_w[...] = down_ref[...].T
-    down_tb[...] = down_w[...].astype(BF16)
+    for c in range(spans):
+        for copy in pair_copies(c, 0):
+            copy.start()
+        if c == 0:
+            for copy in halo:
+                copy.start()
     loads["rate"].wait()
     loads[("k", 0)].wait()
     loads[("v", 0)].wait()
     prepare(0)
+    loads["gate"].wait()
+    start_b[0] = gate_w[...].astype(BF16)
+    loads["up"].wait()
+    start_b[2] = up_w[...].astype(BF16)
+    loads["down"].wait()
+    down_w[...] = down_ref[...].T
+    start_b[1] = down_w[...].astype(BF16)
     loads["ow"].wait()
     if gather_weight:
-        ow_all[span_of(owned(shard, levels - 1), shard), :] = ow_ref[...]
+        ow_all[span_of(owned(shard, levels - 1, 0), shard), :] = ow_ref[...]
         weight_next(levels - 1)
     else:
         ow_t[...] = ow_ref[...]
@@ -397,6 +512,8 @@
 
             work.append(edges)
             work += [functools.partial(attend, s, 0) for s in range(1, spans)]
+        if c + 1 < spans:
+            work.append(functools.partial(prepare_far, c + 1))
         if c > 0:
             work += [functools.partial(apply, c - 1, j) for j in range(tiles)]
         if c == spans - 1:
@@ -411,7 +528,11 @@
                 weight_next(levels - 2)
             gradient(c + 1)
     for j in range(tiles):
-        apply(spans - 1, j)
+        apply_near(spans - 1, j)
+    for j in range(tiles):
+        apply_far(spans - 1, j)
+    for c in range(spans):
+        settle(c)
     for j in range(tiles):
         project(spans - 1, j)
 
@@ -426,13 +547,18 @@
     else:
         weight = lax.all_gather(output_weight, "seq", axis=1, tiled=True).T
     out_cols = shard * n_seq
-    cols = hid // LANES
+    radices = radices_of(n_seq)
+    ways = radices[0]
+    hid_part = hid // ways
+    cols = hid_part // LANES
     total = 3 * cols * dh
-    radices = radices_of(n_seq)
     landing, size = 0, total
-    for radix in radices:
+    for radix in radices[1:]:
         size //= radix
         landing += (radix - 1) * size
+    near_count = ways * max(radices[1:2] + [1])
+    widest = max([near_count] + radices)
+    norms = max(len(radices) - 1, 1)
     slots = sum(radices) + 1
     tiles = rows // WINDOW
     dma = pltpu.SemaphoreType.DMA
@@ -447,32 +573,42 @@
             vmem((spans, rows, dh), BF16),
             vmem((spans, rows, dh), BF16),
             vmem((spans, rows), F32),
-            vmem((dh, hid), F32),
-            vmem((hid, dh), F32),
-            vmem((dh, hid), F32),
+            vmem((dh, hid_part), F32),
+            vmem((hid_part, dh), F32),
+            vmem((dh, hid_part), F32),
             vmem(weight.shape, BF16),
-            vmem((dh, hid), F32),
-            vmem((3, dh, hid), F32),
-            vmem((dh, hid), BF16),
-            vmem((dh, hid), BF16),
-            vmem((dh, hid), BF16),
-            vmem((dh, rows), BF16),
-            vmem((rows, dh), BF16),
-            vmem((dh, rows), BF16),
-            vmem((rows, hid), BF16),
-            vmem((rows, hid), BF16),
-            vmem((rows, hid), BF16),
+            vmem((dh, hid_part), F32),
+            vmem((3, dh, hid_part), F32),
+            vmem((3, dh, hid_part), BF16),
+            vmem((spans, ways, 3, dh, hid_part), BF16),
+            vmem((spans, dh, ways * rows), BF16),
+            vmem((spans, rows, dh), BF16),
+            vmem((spans, dh, ways * rows), BF16),
+            vmem((spans, ways - 1, rows, dh), BF16),
+            vmem((spans, ways - 1, rows, dh), BF16),
+            vmem((ways * rows, hid_part), BF16),
+            vmem((ways * rows, hid_part), BF16),
+            vmem((ways * rows, hid_part), BF16),
             vmem((total, LANES), F32),
             vmem((spans, total, LANES), BF16),
             vmem((spans, landing, LANES), BF16),
             vmem((spans, total, LANES), BF16),
+            vmem((spans, norms, 8, LANES), F32),
+            vmem((spans, norms, widest, 8, LANES), F32),
             vmem((spans, WINDOW, dh), BF16),
             vmem((spans, WINDOW, dh), BF16),
             vmem((out_cols, features), BF16),
             vmem((out_cols, features), BF16),
             vmem((n_head, spans, rows, dh), BF16),
             vmem((spans, rows, dh), F32),
+            vmem((spans, rows, dh), F32),
             dma((6 + 2 * spans,)),
+            dma((spans, 2, ways)),
+            dma((spans, 2, ways)),
+            dma((spans, ways)),
+            dma((spans, ways)),
+            dma((spans, norms, widest)),
+            dma((spans, norms, widest)),
             dma((spans, 3, slots)),
             dma((spans, 3, slots)),
             dma((spans, 3, slots)),

time: 69.8 us -> 71.6 us (1.026)
  Pallas kernels: 67.8 us -> 69.6 us
    pallas_call x1, Pallas kernels: 67.8 us -> 69.6 us  [body(): pl.pallas_call(functools.partial(kernel, n_seq, n_head, gather_weight), o...]
where the time goes in v1:
time: 71.6 us; the launch traced here: 71.5 us
  Pallas kernels  69.6 us (97%)
  local copies, waits for them, and re-layouts  1.87 us (3%)
    pallas_call x1, Pallas kernels, body(): pl.pallas_call(functools.partial(kernel, n_seq, n_head, gather_weight), o...  69.6 us
    unnamed x1, local copies, waits for them, and re-layouts  1.87 us

profile of v1, /device:TPU:0, one launch (start us, length us, event | category | flops | bytes accessed | tf_op | source)
XLA Modules:
  0.0 71.5 jit_solution(6633700209837582877)
XLA Ops:
  0.0 69.6 %shard_map.82 = bf16[2,512,256]{2,1,0:T(8,128)(2,1)} custom-call(bf16[2,512,256]{2,1,0:T(8,128)(2,1)} %bitcast.8, bf16[2,512,256]{2,1,0:T(8,128)(2,1)} %bitcast.9, bf16[2,512,256]{2,1,0:T(8,128)(2,1)} %bitcast.10, f32[2,512]{1,0:T(2,128)} %bitcast.15, f32[256,512]{1,0:T(8,128)} %bitcast.11, f32[512,256]{1,0:T(8,128)} %bitcast.12, f32[256,512]{1,0:T(8,128)} %bitcast.13, ...), custom_call_target="tpu_custom_call" | custom-call | tf_op jit(solution)/shard_map/pallas_call | solution.py:566
  69.6 1.9 %copy.10 = bf16[2,512,256]{2,1,0:T(8,128)(2,1)} copy(bf16[2,512,256]{2,1,0:T(8,128)(2,1)} %shard_map.82) | data formatting | bytes 1048576

commit v2 on v0

--- a/solution.py
+++ b/solution.py
@@ -11,6 +11,7 @@
 WINDOW = 256
 MOMENTUM = 0.9
 LANES = 128
+CHUNK = 16
 MESH = pl.DeviceIdType.MESH
 F32 = jnp.float32
 BF16 = jnp.bfloat16
@@ -47,6 +48,7 @@
     out_ref,
     q_ref, k_ref, v_ref, rate_ref, gate_w, down_ref, up_w, ow_ref, down_w,
     mom, gate_b, up_b, down_tb, keys_t, target, target_t, hid_s, da_s, db_s,
+    gate_f, up_f, back_f, score_f, prob_s, hidden_s, fast_f,
     acc, send_b, recv_b, full_b, edge_k, edge_v, ow_all, ow_t, mix, win,
     load_sem, ar_send, ar_recv, ag_send, ag_recv, halo_send, halo_recv, ow_send, ow_recv, mix_send, mix_recv,
 ):
@@ -123,14 +125,17 @@
         for start in range(0, rows, piece):
             part = slice(start, start + piece)
             k_part = k_ref[c, part]
-            pre_gate = dot(k_part, gate_b[...])
-            pre_up = dot(k_part, up_b[...])
-            back = dot(target[part, :], down_tb[...])
-            sig = sigmoid(pre_gate)
-            silu = pre_gate * sig
-            hid_s[part, :] = (silu * pre_up).astype(BF16)
-            da_s[part, :] = (back * pre_up * (sig * (1.0 + pre_gate * (1.0 - sig)))).astype(BF16)
-            db_s[part, :] = (back * silu).astype(BF16)
+            gate_f[part, :] = dot(k_part, gate_b[...])
+            up_f[part, :] = dot(k_part, up_b[...])
+            back_f[part, :] = dot(target[part, :], down_tb[...])
+            for r in range(start, start + piece, CHUNK):
+                at = slice(r, r + CHUNK)
+                pre_gate, pre_up, back = gate_f[at, :], up_f[at, :], back_f[at, :]
+                sig = sigmoid(pre_gate)
+                silu = pre_gate * sig
+                hid_s[at, :] = (silu * pre_up).astype(BF16)
+                da_s[at, :] = (back * pre_up * (sig * (1.0 + pre_gate * (1.0 - sig)))).astype(BF16)
+                db_s[at, :] = (back * silu).astype(BF16)
         for p, (left, right) in enumerate(((target_t, hid_s), (keys_t, da_s), (keys_t, db_s))):
             grad = dot(left[...], right[...])
             for cb in range(cols):
@@ -251,42 +256,45 @@
             for cb in range(cols):
                 base = p * part_rows + cb * dh
                 lanes = slice(cb * LANES, (cb + 1) * LANES)
-                change = factor * full_b[c, base : base + dh, :].astype(F32)
-                if c > 0:
-                    change = MOMENTUM * mom[m, :, lanes] + change
-                fresh = wts[m][:, lanes] - change
-                if c < spans - 1:
-                    mom[m, :, lanes] = change
-                    wts[m][:, lanes] = fresh
-                current[m][:, lanes] = fresh.astype(BF16)
-
-    row_ids = lax.broadcasted_iota(jnp.int32, (WINDOW, WINDOW), 0)
-    col_ids = lax.broadcasted_iota(jnp.int32, (WINDOW, WINDOW), 1)
+                for r in range(0, dh, 64):
+                    at = slice(r, r + 64)
+                    change = factor * full_b[c, base + r : base + r + 64, :].astype(F32)
+                    if c > 0:
+                        change = MOMENTUM * mom[m, at, lanes] + change
+                    fresh = wts[m][at, lanes] - change
+                    if c < spans - 1:
+                        mom[m, at, lanes] = change
+                        wts[m][at, lanes] = fresh
+                    current[m][at, lanes] = fresh.astype(BF16)
+
     scale = 1.0 / math.sqrt(dh)
 
     def attend(c, j):
         start = j * WINDOW
         here = slice(start, start + WINDOW)
-        left_ok = col_ids > row_ids
         if j == 0:
             first = me == 0
             span = jnp.where(first, (c + spans - 1) % spans, c)
             left_k, left_v = edge_k[span], edge_v[span]
-            if c == 0:
-                left_ok = left_ok & jnp.logical_not(first)
         else:
             earlier = slice(start - WINDOW, start)
             left_k, left_v = k_ref[c, earlier], v_ref[c, earlier]
         query = q_ref[c, here]
-        left = jnp.where(left_ok, dot_t(query, left_k) * scale, -1e30)
-        right = jnp.where(col_ids <= row_ids, dot_t(query, k_ref[c, here]) * scale, -1e30)
-        top = jnp.maximum(jnp.max(left, axis=1, keepdims=True), jnp.max(right, axis=1, keepdims=True))
-        left = jnp.exp(left - top)
-        right = jnp.exp(right - top)
-        share = 1.0 / (jnp.sum(left, axis=1, keepdims=True) + jnp.sum(right, axis=1, keepdims=True))
-        win[c, here] = dot((left * share).astype(BF16), left_v) + dot(
-            (right * share).astype(BF16), v_ref[c, here]
-        )
+        score_f[:, :WINDOW] = dot_t(query, left_k)
+        score_f[:, WINDOW:] = dot_t(query, k_ref[c, here])
+        for r in range(0, WINDOW, CHUNK):
+            at = slice(r, r + CHUNK)
+            row_ids = lax.broadcasted_iota(jnp.int32, (CHUNK, 2 * WINDOW), 0) + r
+            col_ids = lax.broadcasted_iota(jnp.int32, (CHUNK, 2 * WINDOW), 1)
+            lowest = row_ids
+            if j == 0 and c == 0:
+                lowest = jnp.maximum(lowest, jnp.where(me == 0, WINDOW - 1, 0))
+            ok = (col_ids > lowest) & (col_ids <= row_ids + WINDOW)
+            scores = jnp.where(ok, score_f[at, :] * scale, -1e30)
+            scores = jnp.exp(scores - jnp.max(scores, axis=1, keepdims=True))
+            share = 1.0 / jnp.sum(scores, axis=1, keepdims=True)
+            prob_s[at, :] = (scores * share).astype(BF16)
+        win[c, here] = dot(prob_s[:, :WINDOW], left_v) + dot(prob_s[:, WINDOW:], v_ref[c, here])
 
     half = WINDOW
 
@@ -306,11 +314,18 @@
     def apply(c, j):
         part = slice(j * half, (j + 1) * half)
         query = q_ref[c, part]
-        pre_gate = dot(query, gate_b[...])
-        hidden = (pre_gate * sigmoid(pre_gate) * dot(query, up_b[...])).astype(BF16)
-        fast = dot_t(hidden, down_tb[...])
-        norm = fast * lax.rsqrt(jnp.mean(fast * fast, axis=-1, keepdims=True) + 1e-5)
-        mix[head, c, part] = (norm + win[c, part]).astype(BF16)
+        gate_f[part, :] = dot(query, gate_b[...])
+        up_f[part, :] = dot(query, up_b[...])
+        for r in range(0, half, CHUNK):
+            at = slice(j * half + r, j * half + r + CHUNK)
+            pre_gate = gate_f[at, :]
+            hidden_s[r : r + CHUNK, :] = (pre_gate * sigmoid(pre_gate) * up_f[at, :]).astype(BF16)
+        fast_f[...] = dot_t(hidden_s[...], down_tb[...])
+        for r in range(0, half, CHUNK):
+            at = slice(j * half + r, j * half + r + CHUNK)
+            fast = fast_f[r : r + CHUNK, :]
+            norm = fast * lax.rsqrt(jnp.mean(fast * fast, axis=-1, keepdims=True) + 1e-5)
+            mix[head, c, at] = (norm + win[c, at]).astype(BF16)
         for copy in mix_copies(c, j):
             copy.start()
 
@@ -462,6 +477,13 @@
             vmem((rows, hid), BF16),
             vmem((rows, hid), BF16),
             vmem((rows, hid), BF16),
+            vmem((rows, hid), F32),
+            vmem((rows, hid), F32),
+            vmem((rows, hid), F32),
+            vmem((WINDOW, 2 * WINDOW), F32),
+            vmem((WINDOW, 2 * WINDOW), BF16),
+            vmem((WINDOW, hid), BF16),
+            vmem((WINDOW, dh), F32),
             vmem((total, LANES), F32),
             vmem((spans, total, LANES), BF16),
             vmem((spans, landing, LANES), BF16),

time: 69.8 us -> 69.9 us (level)
  no operation moved by 1% of the time
where the time goes in v2:
time: 69.9 us; the launch traced here: 69.8 us
  Pallas kernels  67.9 us (97%)
  local copies, waits for them, and re-layouts  1.87 us (3%)
    pallas_call x1, Pallas kernels, body(): pl.pallas_call(functools.partial(kernel, n_seq, n_head, gather_weight), o...  67.9 us
    unnamed x1, local copies, waits for them, and re-layouts  1.87 us

profile of v2, /device:TPU:0, one launch (start us, length us, event | category | flops | bytes accessed | tf_op | source)
XLA Modules:
  0.0 69.8 jit_solution(2844940415365074969)
XLA Ops:
  0.0 67.9 %shard_map.82 = bf16[2,512,256]{2,1,0:T(8,128)(2,1)} custom-call(bf16[2,512,256]{2,1,0:T(8,128)(2,1)} %bitcast.8, bf16[2,512,256]{2,1,0:T(8,128)(2,1)} %bitcast.9, bf16[2,512,256]{2,1,0:T(8,128)(2,1)} %bitcast.10, f32[2,512]{1,0:T(2,128)} %bitcast.15, f32[256,512]{1,0:T(8,128)} %bitcast.11, f32[512,256]{1,0:T(8,128)} %bitcast.12, f32[256,512]{1,0:T(8,128)} %bitcast.13, ...), custom_call_target="tpu_custom_call" | custom-call | tf_op jit(solution)/shard_map/pallas_call | solution.py:455
  67.9 1.9 %copy.10 = bf16[2,512,256]{2,1,0:T(8,128)(2,1)} copy(bf16[2,512,256]{2,1,0:T(8,128)(2,1)} %shard_map.82) | data formatting | bytes 1048576

commit v3 on v1

--- a/solution.py
+++ b/solution.py
@@ -11,6 +11,8 @@
 WINDOW = 256
 MOMENTUM = 0.9
 LANES = 128
+CHUNK = 16
+PARTS = 2
 MESH = pl.DeviceIdType.MESH
 F32 = jnp.float32
 BF16 = jnp.bfloat16
@@ -29,6 +31,10 @@
     return found
 
 
+def parts_of(rows, holders):
+    return PARTS if rows % (PARTS * holders * 16) == 0 else 1
+
+
 def dot(left, right):
     return jnp.dot(left, right, preferred_element_type=F32)
 
@@ -47,6 +53,7 @@
     out_ref,
     q_ref, k_ref, v_ref, rate_ref, gate_w, down_ref, up_w, ow_ref, down_w,
     mom, start_b, cur, keys_t, target, target_t, k_far, target_far, hid_s, da_s, db_s,
+    gate_f, up_f, back_f, score_f, prob_s, hidden_s, fast_f,
     acc, send_b, recv_b, full_b, sq_out, sq_in, edge_k, edge_v, ow_all, ow_t, mix, win, near,
     load_sem, pair_send, pair_recv, cur_send, cur_recv, sq_send, sq_recv, ar_send, ar_recv, ag_send, ag_recv, halo_send, halo_recv, ow_send, ow_recv, mix_send, mix_recv,
 ):
@@ -55,7 +62,9 @@
     ways = radices_of(n_seq)[0]
     hid_part = hid // ways
     cols = hid_part // LANES
-    part_rows = cols * dh
+    matrix_rows = cols * dh
+    parts = parts_of(3 * matrix_rows, n_seq // ways)
+    part_rows = 3 * matrix_rows // parts
     wts = (gate_w, down_w, up_w)
     radices = radices_of(n_seq)
     levels = len(radices)
@@ -93,13 +102,6 @@
         other = lax.rem(digits[level] + step, radix)
         return me + (other - digits[level]) * strides[level], other
 
-    def near_peer(step):
-        width = ways * radices[1] if levels > 1 else ways
-        spot = lax.rem(me, width)
-        return me + lax.rem(spot + step, width) - spot
-
-    near_steps = range(1, ways * (radices[1] if levels > 1 else 1))
-
     following = lax.rem(me + 1, n_seq)
     before = lax.rem(me + n_seq - 1, n_seq)
 
@@ -109,9 +111,6 @@
         for step in range(1, radices[level]):
             pl.semaphore_signal(barrier, inc=1, device_id={"seq": peer(level, step)[0]}, device_id_type=MESH)
             greeted += 1
-    for step in near_steps:
-        pl.semaphore_signal(barrier, inc=1, device_id={"seq": near_peer(step)}, device_id_type=MESH)
-        greeted += 1
     for other in (following, before):
         pl.semaphore_signal(barrier, inc=1, device_id={"seq": other}, device_id_type=MESH)
         greeted += 1
@@ -165,22 +164,28 @@
                 place = slice(slot * rows + start, slot * rows + start + piece)
                 k_part = k_ref[c, part] if slot == 0 else k_far[c, slot - 1, part]
                 aim = target[c, part] if slot == 0 else target_far[c, slot - 1, part]
-                pre_gate = dot(k_part, weights[0])
-                pre_up = dot(k_part, weights[2])
-                back = dot(aim, weights[1])
-                sig = sigmoid(pre_gate)
-                silu = pre_gate * sig
-                hid_s[place, :] = (silu * pre_up).astype(BF16)
-                da_s[place, :] = (back * pre_up * (sig * (1.0 + pre_gate * (1.0 - sig)))).astype(BF16)
-                db_s[place, :] = (back * silu).astype(BF16)
+                gate_f[place, :] = dot(k_part, weights[0])
+                up_f[place, :] = dot(k_part, weights[2])
+                back_f[place, :] = dot(aim, weights[1])
+                for r in range(place.start, place.start + piece, CHUNK):
+                    at = slice(r, r + CHUNK)
+                    pre_gate, pre_up, back = gate_f[at, :], up_f[at, :], back_f[at, :]
+                    sig = sigmoid(pre_gate)
+                    silu = pre_gate * sig
+                    hid_s[at, :] = (silu * pre_up).astype(BF16)
+                    da_s[at, :] = (back * pre_up * (sig * (1.0 + pre_gate * (1.0 - sig)))).astype(BF16)
+                    db_s[at, :] = (back * silu).astype(BF16)
+        sent = 0
         for p, (left, right) in enumerate(((target_t, hid_s), (keys_t, da_s), (keys_t, db_s))):
             grad = dot(left[c], right[...])
             for cb in range(cols):
-                base = p * part_rows + cb * dh
+                base = p * matrix_rows + cb * dh
                 block = grad[:, cb * LANES : (cb + 1) * LANES]
                 acc[base : base + dh, :] = block
                 send_b[c, base : base + dh, :] = block.astype(BF16)
-            start_stage(c, p, 0)
+            while (sent + 1) * part_rows <= (p + 1) * matrix_rows:
+                start_stage(c, sent, 0)
+                sent += 1
 
     def span_of(start, size):
         return pl.ds(pl.multiple_of(start, 16), size)
@@ -252,7 +257,6 @@
     def finish_stage(c, p, stage):
         for copy in stage_copies(c, p, stage):
             copy.wait_recv()
-        squares = None
         if stage < halfway:
             level = stage + 1
             size = unit * math.prod(radices[level + 1 :])
@@ -268,60 +272,42 @@
                 full_b[c, place, :] = mine.astype(BF16)
         if stage + 1 < stages:
             start_stage(c, p, stage + 1)
-        if stage == halfway - 1:
-            squares = squares_of(mine)
-        return squares
-
-    def norm_copies(c, index):
-        level = levels - 1 - index
+
+    def norm_copies(c):
         made = []
-        for step in range(1, radices[level]) if level > 1 else near_steps:
-            other = peer(level, step)[0] if level > 1 else near_peer(step)
+        for step in range(1, ways):
             made.append(
                 pltpu.make_async_remote_copy(
-                    src_ref=sq_out.at[c, index], dst_ref=sq_in.at[c, index, step],
-                    send_sem=sq_send.at[c, index, step], recv_sem=sq_recv.at[c, index, step],
-                    device_id={"seq": other}, device_id_type=MESH,
+                    src_ref=sq_out.at[c], dst_ref=sq_in.at[c, step],
+                    send_sem=sq_send.at[c, step], recv_sem=sq_recv.at[c, step],
+                    device_id={"seq": peer(0, step)[0]}, device_id_type=MESH,
                 )
             )
         return made
 
-    def norm_start(c, index, squares):
-        sq_out[c, index] = squares
-        for copy in norm_copies(c, index):
-            copy.start()
-
-    def norm_finish(c, index):
-        squares = sq_out[c, index]
-        count = 1
-        for copy in norm_copies(c, index):
-            copy.wait()
-            squares = squares + sq_in[c, index, count]
-            count += 1
-        return squares
-
     def all_reduce(c, work):
-        squares = None
-        for key in range(stages + 2):
+        squares = jnp.zeros((8, LANES), F32)
+        for key in range(stages + parts - 1):
             fill(work)
-            for p in reversed(range(3)):
+            for p in reversed(range(parts)):
                 stage = key - p
                 if 0 <= stage < stages:
-                    term = finish_stage(c, p, stage)
-                    if term is not None:
-                        squares = term if squares is None else squares + term
-            if key >= halfway + 1:
-                index = key - halfway - 1
-                if index > 0:
-                    squares = norm_finish(c, index - 1)
-                if index < halfway:
-                    norm_start(c, index, squares)
+                    finish_stage(c, p, stage)
+                    if stage == stages - 1:
+                        for r in range(p * part_rows, (p + 1) * part_rows, 128):
+                            squares += squares_of(full_b[c, r : r + 128, :].astype(F32))
+        sq_out[c] = squares
+        for copy in norm_copies(c):
+            copy.start()
         while work:
             fill(work)
+        for step, copy in enumerate(norm_copies(c)):
+            copy.wait()
+            squares = squares + sq_in[c, step + 1]
         return squares
 
     def settle(c):
-        for p in range(3):
+        for p in range(parts):
             for stage in range(stages):
                 for copy in stage_copies(c, p, stage):
                     copy.wait_send()
@@ -343,46 +329,49 @@
         factor = jnp.minimum(1.0, 0.6 * math.sqrt(hid) / jnp.sqrt(whole + 1e-6))
         for p, m in ((1, 0), (2, 2), (0, 1)):
             for cb in range(cols):
-                base = p * part_rows + cb * dh
+                base = p * matrix_rows + cb * dh
                 lanes = slice(cb * LANES, (cb + 1) * LANES)
-                change = factor * full_b[c, base : base + dh, :].astype(F32)
-                if c > 0:
-                    change = MOMENTUM * mom[m, :, lanes] + change
-                fresh = wts[m][:, lanes] - change
-                if c < spans - 1:
-                    mom[m, :, lanes] = change
-                    wts[m][:, lanes] = fresh
-                cur[c, 0, m, :, lanes] = fresh.astype(BF16)
+                for r in range(0, dh, 64):
+                    at = slice(r, r + 64)
+                    change = factor * full_b[c, base + r : base + r + 64, :].astype(F32)
+                    if c > 0:
+                        change = MOMENTUM * mom[m, at, lanes] + change
+                    fresh = wts[m][at, lanes] - change
+                    if c < spans - 1:
+                        mom[m, at, lanes] = change
+                        wts[m][at, lanes] = fresh
+                    cur[c, 0, m, at, lanes] = fresh.astype(BF16)
         for copy in cur_copies(c):
             copy.start()
 
-    row_ids = lax.broadcasted_iota(jnp.int32, (WINDOW, WINDOW), 0)
-    col_ids = lax.broadcasted_iota(jnp.int32, (WINDOW, WINDOW), 1)
     scale = 1.0 / math.sqrt(dh)
 
     def attend(c, j):
         start = j * WINDOW
         here = slice(start, start + WINDOW)
-        left_ok = col_ids > row_ids
         if j == 0:
             first = me == 0
             span = jnp.where(first, (c + spans - 1) % spans, c)
             left_k, left_v = edge_k[span], edge_v[span]
-            if c == 0:
-                left_ok = left_ok & jnp.logical_not(first)
         else:
             earlier = slice(start - WINDOW, start)
             left_k, left_v = k_ref[c, earlier], v_ref[c, earlier]
         query = q_ref[c, here]
-        left = jnp.where(left_ok, dot_t(query, left_k) * scale, -1e30)
-        right = jnp.where(col_ids <= row_ids, dot_t(query, k_ref[c, here]) * scale, -1e30)
-        top = jnp.maximum(jnp.max(left, axis=1, keepdims=True), jnp.max(right, axis=1, keepdims=True))
-        left = jnp.exp(left - top)
-        right = jnp.exp(right - top)
-        share = 1.0 / (jnp.sum(left, axis=1, keepdims=True) + jnp.sum(right, axis=1, keepdims=True))
-        win[c, here] = dot((left * share).astype(BF16), left_v) + dot(
-            (right * share).astype(BF16), v_ref[c, here]
-        )
+        score_f[:, :WINDOW] = dot_t(query, left_k)
+        score_f[:, WINDOW:] = dot_t(query, k_ref[c, here])
+        for r in range(0, WINDOW, CHUNK):
+            at = slice(r, r + CHUNK)
+            row_ids = lax.broadcasted_iota(jnp.int32, (CHUNK, 2 * WINDOW), 0) + r
+            col_ids = lax.broadcasted_iota(jnp.int32, (CHUNK, 2 * WINDOW), 1)
+            lowest = row_ids
+            if j == 0 and c == 0:
+                lowest = jnp.maximum(lowest, jnp.where(me == 0, WINDOW - 1, 0))
+            ok = (col_ids > lowest) & (col_ids <= row_ids + WINDOW)
+            scores = jnp.where(ok, score_f[at, :] * scale, -1e30)
+            scores = jnp.exp(scores - jnp.max(scores, axis=1, keepdims=True))
+            share = 1.0 / jnp.sum(scores, axis=1, keepdims=True)
+            prob_s[at, :] = (scores * share).astype(BF16)
+        win[c, here] = dot(prob_s[:, :WINDOW], left_v) + dot(prob_s[:, WINDOW:], v_ref[c, here])
 
     half = WINDOW
 
@@ -401,9 +390,13 @@
 
     def fast_part(c, j, slot):
         query = q_ref[c, j * half : (j + 1) * half]
-        pre_gate = dot(query, cur[c, slot, 0])
-        hidden = (pre_gate * sigmoid(pre_gate) * dot(query, cur[c, slot, 2])).astype(BF16)
-        return dot_t(hidden, cur[c, slot, 1])
+        gate_f[:half, :] = dot(query, cur[c, slot, 0])
+        up_f[:half, :] = dot(query, cur[c, slot, 2])
+        for r in range(0, half, CHUNK):
+            at = slice(r, r + CHUNK)
+            pre_gate = gate_f[at, :]
+            hidden_s[at, :] = (pre_gate * sigmoid(pre_gate) * up_f[at, :]).astype(BF16)
+        return dot_t(hidden_s[...], cur[c, slot, 1])
 
     def apply_near(c, j):
         near[c, j * half : (j + 1) * half] = fast_part(c, j, 0)
@@ -413,11 +406,13 @@
         if j == 0:
             for copy in cur_copies(c):
                 copy.wait()
-        fast = near[c, part]
         for slot in range(1, ways):
-            fast = fast + fast_part(c, j, slot)
-        norm = fast * lax.rsqrt(jnp.mean(fast * fast, axis=-1, keepdims=True) + 1e-5)
-        mix[head, c, part] = (norm + win[c, part]).astype(BF16)
+            near[c, part] += fast_part(c, j, slot)
+        for r in range(0, half, CHUNK):
+            at = slice(j * half + r, j * half + r + CHUNK)
+            fast = near[c, at]
+            norm = fast * lax.rsqrt(jnp.mean(fast * fast, axis=-1, keepdims=True) + 1e-5)
+            mix[head, c, at] = (norm + win[c, at]).astype(BF16)
         for copy in mix_copies(c, j):
             copy.start()
 
@@ -531,10 +526,10 @@
         apply_near(spans - 1, j)
     for j in range(tiles):
         apply_far(spans - 1, j)
+    for j in range(tiles):
+        project(spans - 1, j)
     for c in range(spans):
         settle(c)
-    for j in range(tiles):
-        project(spans - 1, j)
 
 
 def body(n_seq, n_head, queries, key_rows, values, learn_rates, fast_gate, fast_down, fast_up, output_weight):
@@ -556,9 +551,7 @@
     for radix in radices[1:]:
         size //= radix
         landing += (radix - 1) * size
-    near_count = ways * max(radices[1:2] + [1])
-    widest = max([near_count] + radices)
-    norms = max(len(radices) - 1, 1)
+    parts = parts_of(total, n_seq // ways)
     slots = sum(radices) + 1
     tiles = rows // WINDOW
     dma = pltpu.SemaphoreType.DMA
@@ -589,12 +582,19 @@
             vmem((ways * rows, hid_part), BF16),
             vmem((ways * rows, hid_part), BF16),
             vmem((ways * rows, hid_part), BF16),
+            vmem((ways * rows, hid_part), F32),
+            vmem((ways * rows, hid_part), F32),
+            vmem((ways * rows, hid_part), F32),
+            vmem((WINDOW, 2 * WINDOW), F32),
+            vmem((WINDOW, 2 * WINDOW), BF16),
+            vmem((WINDOW, hid_part), BF16),
+            vmem((WINDOW, dh), F32),
             vmem((total, LANES), F32),
             vmem((spans, total, LANES), BF16),
             vmem((spans, landing, LANES), BF16),
             vmem((spans, total, LANES), BF16),
-            vmem((spans, norms, 8, LANES), F32),
-            vmem((spans, norms, widest, 8, LANES), F32),
+            vmem((spans, 8, LANES), F32),
+            vmem((spans, ways, 8, LANES), F32),
             vmem((spans, WINDOW, dh), BF16),
             vmem((spans, WINDOW, dh), BF16),
             vmem((out_cols, features), BF16),
@@ -607,12 +607,12 @@
             dma((spans, 2, ways)),
             dma((spans, ways)),
             dma((spans, ways)),
-            dma((spans, norms, widest)),
-            dma((spans, norms, widest)),
-            dma((spans, 3, slots)),
-            dma((spans, 3, slots)),
-            dma((spans, 3, slots)),
-            dma((spans, 3, slots)),
+            dma((spans, ways)),
+            dma((spans, ways)),
+            dma((spans, parts, slots)),
+            dma((spans, parts, slots)),
+            dma((spans, parts, slots)),
+            dma((spans, parts, slots)),
             dma((2, spans)),
             dma((2, spans)),
             dma((slots,)),

time: 71.6 us -> 67.3 us (0.940)
  Pallas kernels: 69.6 us -> 64.7 us
    pallas_call x1, Pallas kernels: 69.6 us -> 64.7 us  [body(): pl.pallas_call(functools.partial(kernel, n_seq, n_head, gather_weight), o...]
where the time goes in v3:
time: 67.3 us; the launch traced here: 66.6 us
  Pallas kernels  64.7 us (96%)
  local copies, waits for them, and re-layouts  1.87 us (3%)
    pallas_call x1, Pallas kernels, body(): pl.pallas_call(functools.partial(kernel, n_seq, n_head, gather_weight), o...  64.7 us
    unnamed x1, local copies, waits for them, and re-layouts  1.87 us

profile of v3, /device:TPU:0, one launch (start us, length us, event | category | flops | bytes accessed | tf_op | source)
XLA Modules:
  0.0 66.6 jit_solution(7604674648237802605)
XLA Ops:
  0.0 64.7 %shard_map.82 = bf16[2,512,256]{2,1,0:T(8,128)(2,1)} custom-call(bf16[2,512,256]{2,1,0:T(8,128)(2,1)} %bitcast.8, bf16[2,512,256]{2,1,0:T(8,128)(2,1)} %bitcast.9, bf16[2,512,256]{2,1,0:T(8,128)(2,1)} %bitcast.10, f32[2,512]{1,0:T(2,128)} %bitcast.15, f32[256,512]{1,0:T(8,128)} %bitcast.11, f32[512,256]{1,0:T(8,128)} %bitcast.12, f32[256,512]{1,0:T(8,128)} %bitcast.13, ...), custom_call_target="tpu_custom_call" | custom-call | tf_op jit(solution)/shard_map/pallas_call | solution.py:559
  64.7 1.9 %copy.10 = bf16[2,512,256]{2,1,0:T(8,128)(2,1)} copy(bf16[2,512,256]{2,1,0:T(8,128)(2,1)} %shard_map.82) | data formatting | bytes 1048576
